TPU v7x, 32 devices: a whole 2x2x4 slice. The times are simulated.
32 devices in a mesh: req: 4 (over y, x), patch: 8 (over z, core).
Axes of the slice: x: 2, y: 2, z: 4, core: 2. Of those that a mesh axis runs over, the one named last changes fastest.
Arguments:
- field: float32 [64, 16, 640], P(('req', 'patch')), parts along dimension 0
- stale_conv_in: bfloat16 [64, 16, 640], P(('req', 'patch')), parts along dimension 0, may hold values from -6 to 6
- stale_keys: bfloat16 [1024, 320], P(('req', 'patch')), parts along dimension 0, may hold values from -6 to 6
- stale_values: bfloat16 [1024, 320], P(('req', 'patch')), parts along dimension 0, may hold values from -6 to 6
- norm1_gain: float32 [640], replicated, may hold values from 0.25 to 1.75
- norm1_bias: float32 [640], replicated, may hold values from -3 to 3
- conv_weight: bfloat16 [3, 3, 640, 640], P(None, None, None, 'patch'), may hold values from -0.078125 to 0.078125
- conv_bias: float32 [640], replicated, may hold values from -3 to 3
- time_embed: float32 [8, 640], P('req'), parts along dimension 0, may hold values from -5 to 5
- norm2_gain: float32 [640], replicated, may hold values from 0.25 to 1.75
- norm2_bias: float32 [640], replicated, may hold values from -3 to 3
- w_query: bfloat16 [640, 320], replicated
- w_keyvalue: bfloat16 [640, 640], replicated, may hold values from -0.25 to 0.25
- w_out: bfloat16 [320, 640], replicated, may hold values from -0.3125 to 0.3125
Outputs:
- outputs: float32 [2, 64, 16, 640], P(None, ('req', 'patch')), parts along dimension 1
There are 4 independent parts, one for each index of `req`. A program takes and returns all parts, laid end to end along the dimension named above; an argument that names none is the same for every part. Nothing has to cross between parts.
All inputs are finite; a program needn't handle non-finite values.
Results may differ from a plain program's by a relative error of at most 0.0047.
Values may be sent and summed in bfloat16 or wider, within the bound.
A program may use at most 64 MiB of HBM per device.

v0:
```python
import jax
import jax.numpy as jnp
from jax import lax
from jax.sharding import PartitionSpec as P

GROUPS = 32
HEADS = 5
HEAD_DIM = 64


epsilon = 1e-05


def group_norm(values_in, gain, bias):
    members = values_in.shape[2] // GROUPS
    grouped = values_in.reshape(-1, GROUPS, members)
    totals, squares = lax.psum(
        (jnp.sum(grouped, axis=(0, 2)), jnp.sum(grouped * grouped, axis=(0, 2))), "patch"
    )
    number = grouped.shape[0] * lax.axis_size("patch") * members
    average = totals / number
    variance = squares / number - average * average
    scaled = (grouped - average[None, :, None]) * lax.rsqrt(variance + epsilon)[None, :, None]
    return scaled.reshape(values_in.shape) * gain + bias


def build_blocks(current_all, previous_all, parts):
    blocks = current_all.reshape(parts, -1, current_all.shape[1], current_all.shape[2])
    prior_blocks = previous_all.reshape(blocks.shape)
    zero_row = jnp.zeros_like(blocks[:1, :1])
    above = jnp.concatenate([zero_row, prior_blocks[:-1, -1:]], axis=0)
    below = jnp.concatenate([prior_blocks[1:, :1], zero_row], axis=0)
    stacked = jnp.concatenate([above, blocks, below], axis=1)
    return jnp.pad(stacked, ((0, 0), (0, 0), (1, 1), (0, 0)))


def conv_rows(padded, kernel):
    inner = padded.shape[1] - 2
    across = padded.shape[2] - 2
    result = None
    for offset_row in range(3):
        for offset_col in range(3):
            window = padded[:, offset_row : offset_row + inner, offset_col : offset_col + across, :]
            window = window.reshape(-1, padded.shape[3])
            term = jnp.dot(
                window, kernel[offset_row, offset_col], preferred_element_type=jnp.float32
            )
            result = term if result is None else result + term
    return result


def attend(normed, w_query, w_keyvalue, w_out, prior_keys, prior_values):
    key_width = w_query.shape[1]
    own_rows = normed.shape[0]
    query = jnp.dot(normed, w_query, preferred_element_type=jnp.float32).astype(jnp.bfloat16)
    keyvalue = jnp.dot(normed, w_keyvalue, preferred_element_type=jnp.float32).astype(jnp.bfloat16)
    keys = keyvalue[:, :key_width]
    values = keyvalue[:, key_width:]
    all_keys, all_values = (
        lax.all_gather(prior_keys, "patch", axis=0, tiled=True),
        lax.all_gather(prior_values, "patch", axis=0, tiled=True),
    )
    start = lax.axis_index("patch") * own_rows
    all_keys = lax.dynamic_update_slice_in_dim(all_keys, keys, start, 0)
    all_values = lax.dynamic_update_slice_in_dim(all_values, values, start, 0)
    query_heads = query.reshape(own_rows, HEADS, HEAD_DIM)
    key_heads = all_keys.reshape(-1, HEADS, HEAD_DIM)
    value_heads = all_values.reshape(-1, HEADS, HEAD_DIM)
    scores = jnp.einsum(
        "qhd,khd->hqk", query_heads, key_heads, preferred_element_type=jnp.float32
    ) * HEAD_DIM ** (-0.5)
    peak = jnp.max(scores, axis=-1, keepdims=True)
    expo = jnp.exp(scores - peak)
    totals = jnp.sum(expo, axis=-1, keepdims=True)
    weights = expo.astype(jnp.bfloat16)
    summed = (
        jnp.einsum("hqk,khd->hqd", weights, value_heads, preferred_element_type=jnp.float32)
        / totals
    )
    attended = summed.transpose(1, 0, 2).reshape(own_rows, key_width).astype(jnp.bfloat16)
    mixed = jnp.dot(attended, w_out, preferred_element_type=jnp.float32)
    return (mixed, keys, values)


def per_device(
    field,
    stale_conv_in,
    stale_keys,
    stale_values,
    norm1_gain,
    norm1_bias,
    conv_weight,
    conv_bias,
    time_embed,
    norm2_gain,
    norm2_bias,
    w_query,
    w_keyvalue,
    w_out,
):
    parts = lax.axis_size("patch")
    channels = field.shape[2]
    state = field
    prior_keys = stale_keys
    prior_values = stale_values
    prior_whole = lax.all_gather(stale_conv_in, "patch", axis=0, tiled=True)
    results = []
    for which_step in range(2):
        activated = jax.nn.silu(group_norm(state, norm1_gain, norm1_bias)).astype(jnp.bfloat16)
        current_whole = lax.all_gather(activated, "patch", axis=0, tiled=True)
        padded = build_blocks(current_whole, prior_whole, parts)
        partial_out = conv_rows(padded, conv_weight)
        conv_out = lax.all_to_all(
            partial_out, "patch", split_axis=0, concat_axis=1, tiled=True
        ).reshape(state.shape)
        prior_whole = current_whole
        hidden = state + (conv_out + conv_bias + time_embed[which_step])
        normed = (
            group_norm(hidden, norm2_gain, norm2_bias).astype(jnp.bfloat16).reshape(-1, channels)
        )
        mixed, prior_keys, prior_values = attend(
            normed, w_query, w_keyvalue, w_out, prior_keys, prior_values
        )
        result = hidden + mixed.reshape(hidden.shape)
        results.append(result)
        state = result
    return jnp.stack(results)


def solution(mesh):
    placed = (
        P(("req", "patch"), None, None),
        P(("req", "patch"), None, None),
        P(("req", "patch"), None),
        P(("req", "patch"), None),
        P(),
        P(),
        P(None, None, None, "patch"),
        P(),
        P("req", None),
        P(),
        P(),
        P(),
        P(),
        P(),
    )
    return jax.shard_map(
        per_device,
        mesh=mesh,
        in_specs=placed,
        out_specs=P(None, ("req", "patch"), None, None),
        check_vma=False,
    )
```

profile of v0, /device:TPU:1, one launch (start us, length us, event | category | flops | bytes accessed | tf_op | source)
XLA Modules:
  0.0 191.7 jit_solution(16671620254477837993)
XLA Ops:
  0.0 16.3 %all_gather.21 = bf16[16,16,640]{2,1,0:T(8,128)(2,1)S(1)} all-gather(bf16[2,16,640]{2,1,0:T(8,128)(2,1)} %param.15), channel_id=1, replica_groups=mesh['req'=4,'patch'=8] {'patch'}, dimensions={0}, use_global_device_ids=true | all-gather | bytes 368640 | tf_op jit(solution)/shard_map/all_gather | solution.py:106
  16.5 0.1 reduce_sum.119
  16.7 0.1 reduce_sum.113
  16.8 13.1 %all-reduce.9 = (f32[32]{0:T(128)S(1)}, f32[32]{0:T(128)S(1)}) all-reduce(f32[32]{0:T(128)S(1)} %reduce_sum.119, f32[32]{0:T(128)S(1)} %reduce_sum.113), channel_id=1, replica_groups=mesh['req'=4,'patch'=8] {'patch'}, use_global_device_ids=true, to_apply=%region_5.6 | all-reduce | flops 64 | bytes 512 | tf_op jit(solution)/shard_map/psum | solution.py:17
  30.3 18.2 %all_gather.22 = bf16[16,16,640]{2,1,0:T(8,128)(2,1)S(1)} all-gather(bf16[2,16,640]{2,1,0:T(8,128)(2,1)S(1)} %multiply_convert_fusion.1), channel_id=1, replica_groups=mesh['req'=4,'patch'=8] {'patch'}, dimensions={0}, use_global_device_ids=true | all-gather | bytes 368640 | tf_op jit(solution)/shard_map/all_gather | solution.py:110
  48.6 0.4 select_maximum_fusion.2
  49.1 0.3 fusion.62
  49.4 0.9 copy-done.1
  50.3 0.2 fusion.31
  50.5 0.2 convolution_add_fusion.17
  50.8 0.2 convolution_add_fusion.16
  51.0 0.2 convolution_add_fusion.15
  51.3 0.2 convolution_add_fusion.14
  51.5 0.2 convolution_add_fusion.13
  51.8 0.2 convolution_add_fusion.12
  52.0 0.2 convolution_add_fusion.11
  52.3 0.2 convolution_add_fusion.10
  52.5 0.7 copy.37
  53.3 3.4 %all-to-all-start = ((f32[8,32,80]{2,1,0:T(8,128)}), f32[8,32,80]{2,1,0:T(8,128)S(1)}, u32[]{:S(2)}, u32[]{:S(2)}) async-start(f32[8,32,80]{2,1,0:T(8,128)} %bitcast.20), calls=%async_computation | async-start | bytes 262144 | tf_op jit(solution)/shard_map/all_to_all | solution.py:113
  56.7 15.3 %all_gather.24 = bf16[256,320]{1,0:T(8,128)(2,1)S(1)} all-gather(bf16[32,320]{1,0:T(8,128)(2,1)S(1)} %copy-done.5), channel_id=1, replica_groups=mesh['req'=4,'patch'=8] {'patch'}, dimensions={0}, use_global_device_ids=true | all-gather | bytes 184320 | tf_op jit(solution)/shard_map/all_gather | solution.py:61
  72.0 14.2 %all_gather.23 = bf16[256,320]{1,0:T(8,128)(2,1)S(1)} all-gather(bf16[32,320]{1,0:T(8,128)(2,1)S(1)} %copy-done.6), channel_id=1, replica_groups=mesh['req'=4,'patch'=8] {'patch'}, dimensions={0}, use_global_device_ids=true | all-gather | bytes 184320 | tf_op jit(solution)/shard_map/all_gather | solution.py:60
  86.2 0.8 copy.42
  87.0 0.1 copy.39
  87.6 0.1 reduce_sum.128
  87.8 0.1 reduce_sum.122
  87.9 13.1 %all-reduce.8 = (f32[32]{0:T(128)S(1)}, f32[32]{0:T(128)S(1)}) all-reduce(f32[32]{0:T(128)S(1)} %reduce_sum.128, f32[32]{0:T(128)S(1)} %reduce_sum.122), channel_id=1, replica_groups=mesh['req'=4,'patch'=8] {'patch'}, use_global_device_ids=true, to_apply=%region_11.12 | all-reduce | flops 64 | bytes 512 | tf_op jit(solution)/shard_map/psum | solution.py:17
  101.5 0.3 convolution_convert_fusion.1
  101.8 0.1 copy.43
  102.0 0.1 copy.40
  102.1 0.2 convolution_convert_fusion.3
  102.5 2.0 %dynamic_update_slice.13 = bf16[256,320]{0,1:T(8,128)(2,1)} dynamic-update-slice(bf16[256,320]{0,1:T(8,128)(2,1)} %copy.42, bf16[32,320]{0,1:T(8,128)(2,1)S(1)} %copy.43, s32[]{:T(128)S(6)} %select_n.2, s32[]{:T(128)} %constant.31.clone.1) | dynamic-update-slice | bytes 40964 | tf_op jit(solution)/shard_map/dynamic_update_slice | solution.py:65
  104.5 0.7 dynamic_update_slice.12
  105.1 0.2 fusion.66
  105.4 0.2 fusion.9
  105.5 1.2 fusion.4
  106.8 0.2 fusion.58
  107.4 0.1 reduce_sum.161
  107.5 15.6 %all-reduce.7 = (f32[32]{0:T(128)S(1)}, f32[32]{0:T(128)S(1)}) all-reduce(f32[32]{0:T(128)S(1)} %reduce_sum.164, f32[32]{0:T(128)S(1)} %reduce_sum.161), channel_id=1, replica_groups=mesh['req'=4,'patch'=8] {'patch'}, use_global_device_ids=true, to_apply=%region_19.20 | all-reduce | flops 64 | bytes 512 | tf_op jit(solution)/shard_map/psum | solution.py:17
  123.5 14.8 %all_gather.25 = bf16[16,16,640]{2,1,0:T(8,128)(2,1)S(1)} all-gather(bf16[2,16,640]{2,1,0:T(8,128)(2,1)S(1)} %multiply_convert_fusion), channel_id=1, replica_groups=mesh['req'=4,'patch'=8] {'patch'}, dimensions={0}, use_global_device_ids=true | all-gather | bytes 368640 | tf_op jit(solution)/shard_map/all_gather | solution.py:110
  138.3 0.4 select_maximum_fusion
  138.8 0.3 fusion.61
  139.1 0.2 fusion.29
  139.3 0.2 convolution_add_fusion.8
  139.6 0.2 convolution_add_fusion.7
  139.8 0.2 convolution_add_fusion.6
  140.0 0.2 convolution_add_fusion.5
  140.3 0.2 convolution_add_fusion.4
  140.5 0.2 convolution_add_fusion.3
  140.8 0.2 convolution_add_fusion.2
  141.0 0.2 convolution_add_fusion.1
  141.3 0.8 copy.45
  142.0 3.4 %all-to-all-start.1 = ((f32[8,32,80]{2,1,0:T(8,128)}), f32[8,32,80]{2,1,0:T(8,128)S(1)}, u32[]{:S(2)}, u32[]{:S(2)}) async-start(f32[8,32,80]{2,1,0:T(8,128)} %bitcast.39), calls=%async_computation.1 | async-start | bytes 262144 | tf_op jit(solution)/shard_map/all_to_all | solution.py:113
  145.5 15.3 %all_gather.26 = bf16[256,320]{1,0:T(8,128)(2,1)S(1)} all-gather(bf16[32,320]{1,0:T(8,128)(2,1)S(1)} %get-tuple-element.47), channel_id=1, replica_groups=mesh['req'=4,'patch'=8] {'patch'}, dimensions={0}, use_global_device_ids=true | all-gather | bytes 184320 | tf_op jit(solution)/shard_map/all_gather | solution.py:60
  160.8 14.1 %all_gather.27 = bf16[256,320]{1,0:T(8,128)(2,1)S(1)} all-gather(bf16[32,320]{1,0:T(8,128)(2,1)S(1)} %get-tuple-element.48), channel_id=1, replica_groups=mesh['req'=4,'patch'=8] {'patch'}, dimensions={0}, use_global_device_ids=true | all-gather | bytes 184320 | tf_op jit(solution)/shard_map/all_gather | solution.py:61
  175.5 13.1 %all-reduce.6 = (f32[32]{0:T(128)S(1)}, f32[32]{0:T(128)S(1)}) all-reduce(f32[32]{0:T(128)S(1)} %reduce_sum.170, f32[32]{0:T(128)S(1)} %reduce_sum.167), channel_id=1, replica_groups=mesh['req'=4,'patch'=8] {'patch'}, use_global_device_ids=true, to_apply=%region_25.26 | all-reduce | flops 64 | bytes 512 | tf_op jit(solution)/shard_map/psum | solution.py:17
  189.1 0.2 convolution_convert_fusion
  189.3 0.2 convolution_convert_fusion.2
  189.7 0.1 copy.49
  189.8 0.1 copy.47
  190.0 0.2 fusion.67
  190.3 0.2 fusion.11
  190.4 0.2 fusion.5
  190.8 0.2 fusion.3
  191.0 0.7 pad_maximum_fusion.4
  (86 shorter events, 4.1 us)
Async XLA Ops:
  0.0 101.5 %copy-start = (bf16[640,640]{1,0:T(8,128)(2,1)S(1)}, bf16[640,640]{1,0:T(8,128)(2,1)}, u32[]{:S(2)}) copy-start(bf16[640,640]{1,0:T(8,128)(2,1)} %param.26) | copy-start | bytes 2457604
  0.0 16.3 %copy-start.4 = (f32[2,16,640]{2,1,0:T(8,128)S(1)}, f32[2,16,640]{2,1,0:T(8,128)}, u32[]{:S(2)}) copy-start(f32[2,16,640]{2,1,0:T(8,128)} %param.14) | copy-start | bytes 245764
  0.0 30.3 %copy-start.8 = (f32[640]{0:T(1024)S(1)}, f32[640]{0:T(1024)}, u32[]{:S(2)}) copy-start(f32[640]{0:T(1024)} %param.19) | copy-start | bytes 7684
  0.0 30.3 %copy-start.9 = (f32[640]{0:T(1024)S(1)}, f32[640]{0:T(1024)}, u32[]{:S(2)}) copy-start(f32[640]{0:T(1024)} %param.18) | copy-start | bytes 7684
  49.1 1.2 copy-start.1
  52.0 4.7 %copy-start.5 = (bf16[32,320]{1,0:T(8,128)(2,1)S(1)}, bf16[32,320]{1,0:T(8,128)(2,1)}, u32[]{:S(2)}) copy-start(bf16[32,320]{1,0:T(8,128)(2,1)} %param.17) | copy-start | bytes 61444
  52.3 19.8 %copy-start.6 = (bf16[32,320]{1,0:T(8,128)(2,1)S(1)}, bf16[32,320]{1,0:T(8,128)(2,1)}, u32[]{:S(2)}) copy-start(bf16[32,320]{1,0:T(8,128)(2,1)} %param.16) | copy-start | bytes 61444
  53.3 34.0 %all-to-all-start = ((f32[8,32,80]{2,1,0:T(8,128)}), f32[8,32,80]{2,1,0:T(8,128)S(1)}, u32[]{:S(2)}, u32[]{:S(2)}) async-start(f32[8,32,80]{2,1,0:T(8,128)} %bitcast.20), calls=%async_computation | async-start | bytes 262144 | tf_op jit(solution)/shard_map/all_to_all | solution.py:113
  56.7 30.5 %copy-start.12 = (f32[2,640]{1,0:T(2,128)S(1)}, f32[2,640]{1,0:T(2,128)}, u32[]{:S(2)}) copy-start(f32[2,640]{1,0:T(2,128)} %param.22) | copy-start | bytes 15364
  72.0 15.4 %copy-start.7 = (f32[640]{0:T(1024)S(1)}, f32[640]{0:T(1024)}, u32[]{:S(2)}) copy-start(f32[640]{0:T(1024)} %param.21) | copy-start | bytes 7684
  87.0 14.4 %copy-start.10 = (f32[640]{0:T(1024)S(1)}, f32[640]{0:T(1024)}, u32[]{:S(2)}) copy-start(f32[640]{0:T(1024)} %param.24) | copy-start | bytes 7684
  87.0 14.4 %copy-start.11 = (f32[640]{0:T(1024)S(1)}, f32[640]{0:T(1024)}, u32[]{:S(2)}) copy-start(f32[640]{0:T(1024)} %param.23) | copy-start | bytes 7684
  87.3 14.8 %copy-start.3 = (bf16[640,320]{0,1:T(8,128)(2,1)S(1)}, bf16[640,320]{0,1:T(8,128)(2,1)}, u32[]{:S(2)}) copy-start(bf16[640,320]{0,1:T(8,128)(2,1)} %param.25) | copy-start | bytes 1228804
  102.1 4.7 %copy-start.2 = (bf16[320,640]{1,0:T(8,128)(2,1)S(1)}, bf16[320,640]{1,0:T(8,128)(2,1)}, u32[]{:S(2)}) copy-start(bf16[320,640]{1,0:T(8,128)(2,1)} %param.27) | copy-start | bytes 1228804
  142.0 32.8 %all-to-all-start.1 = ((f32[8,32,80]{2,1,0:T(8,128)}), f32[8,32,80]{2,1,0:T(8,128)S(1)}, u32[]{:S(2)}, u32[]{:S(2)}) async-start(f32[8,32,80]{2,1,0:T(8,128)} %bitcast.39), calls=%async_computation.1 | async-start | bytes 262144 | tf_op jit(solution)/shard_map/all_to_all | solution.py:113
where the time goes:
time: 195 us; the launch traced here: 192 us
  blocking collectives  163 us (84%)
  local copies, waits for them, and re-layouts  10.4 us (5%)
  matrix products  7.47 us (4%)
  starting transfers between devices  6.88 us (4%)
  other arithmetic  3.21 us (2%)
    psum x4, blocking collectives, group_norm(): lax.psum((jnp.sum(grouped, axis=(0, 2)), jnp.sum(grouped * grouped, axis=...  54.9 us
    all_gather x2, blocking collectives, per_device(): current_whole = lax.all_gather(activated, 'patch', axis=0, tiled=True)  33 us
    all_gather x2, blocking collectives, attend(): lax.all_gather(prior_keys, 'patch', axis=0, tiled=True)  29.5 us
    all_gather x2, blocking collectives, attend(): lax.all_gather(prior_values, 'patch', axis=0, tiled=True)  29.4 us
    all_gather x1, blocking collectives, per_device(): prior_whole = lax.all_gather(stale_conv_in, 'patch', axis=0, tiled=True)  16.3 us
    all_to_all x2, starting transfers between devices, per_device(): lax.all_to_all(partial_out, 'patch', split_axis=0, concat_axis=1, tiled=T...  6.88 us
    dot_general x18, matrix products, conv_rows(): jnp.dot(window, kernel[offset_row, offset_col], preferred_element_type=jn...  4.27 us
  transfers between devices with their start and end apart: 2, of which 0 were waited for; matrix products, arithmetic and copies ran while one was open for 1% of the time, Pallas kernels for 0%

commit v1 on v0

v1 whole, which is shorter than its diff:
```python
import functools

import jax
import jax.numpy as jnp
import numpy as np
from jax import lax
from jax.experimental import pallas as pl
from jax.experimental.pallas import tpu as pltpu
from jax.sharding import PartitionSpec as P

GROUPS = 32
HEADS = 5
HEAD_DIM = 64
LANES = 128
STEPS = 2
CORES = 2

epsilon = 1e-05
MESH = pl.DeviceIdType.MESH
F32 = jnp.float32
BF16 = jnp.bfloat16


def split_rows(pair):
    high = pair.astype(BF16).astype(F32)
    rest = pair - high
    middle = rest.astype(BF16).astype(F32)
    return jnp.concatenate([high, middle, rest - middle], axis=0).astype(BF16)


def exact_dot(pair, zero_one):
    rows = pair.shape[0]
    product = jnp.dot(split_rows(pair), zero_one, preferred_element_type=F32)
    return product[:rows] + product[rows : 2 * rows] + product[2 * rows :]


def moments(values):
    return jnp.concatenate(
        [
            jnp.sum(values, axis=0, keepdims=True),
            jnp.sum(values * values, axis=0, keepdims=True),
        ],
        axis=0,
    )


def mean_and_scale(sums, number):
    average = sums[0:1] * (1.0 / number)
    variance = sums[1:2] * (1.0 / number) - average * average
    return average, lax.rsqrt(variance + epsilon)


class Gather:
    def __init__(self, parts, me, source, target, send, recv, forward_send, forward_recv):
        self.chips = parts // CORES
        self.me = me
        self.chip, self.core = me // CORES, me % CORES
        self.twin = self.chip * CORES + (1 - self.core)
        self.source, self.target = source, target
        self.sems = (send, recv, forward_send, forward_recv)

    def first(self, distance):
        send, recv, _, _ = self.sems
        peer = (
            self.twin
            if distance == 0
            else lax.rem(self.chip + distance, self.chips) * CORES + self.core
        )
        return pltpu.make_async_remote_copy(
            src_ref=self.source,
            dst_ref=self.target.at[self.me],
            send_sem=send.at[distance],
            recv_sem=recv.at[distance],
            device_id={"patch": peer},
            device_id_type=MESH,
        )

    def second(self, distance):
        _, _, send, recv = self.sems
        origin = lax.rem(self.chip - distance + self.chips, self.chips) * CORES + self.core
        return pltpu.make_async_remote_copy(
            src_ref=self.target.at[origin],
            dst_ref=self.target.at[origin],
            send_sem=send.at[distance],
            recv_sem=recv.at[distance],
            device_id={"patch": self.twin},
            device_id_type=MESH,
        )

    def start(self):
        for distance in list(range(1, self.chips)) + [0]:
            self.first(distance).start()

    def forward(self):
        for distance in range(1, self.chips):
            self.first(distance).wait_recv()
            self.second(distance).start()

    def arrive(self):
        self.first(0).wait_recv()
        for distance in range(1, self.chips):
            self.second(distance).wait_recv()

    def drain(self):
        for distance in range(self.chips):
            self.first(distance).wait_send()
        for distance in range(1, self.chips):
            self.second(distance).wait_send()


class Exchange:
    def __init__(self, parts, me, source, target, send, recv, shared=False):
        self.parts, self.me = parts, me
        self.source, self.target = source, target
        self.send, self.recv, self.shared = send, recv, shared

    def copy(self, distance):
        peer = lax.rem(self.me + distance, self.parts)
        return pltpu.make_async_remote_copy(
            src_ref=self.source if self.shared else self.source.at[peer],
            dst_ref=self.target.at[self.me],
            send_sem=self.send.at[distance],
            recv_sem=self.recv.at[distance],
            device_id={"patch": peer},
            device_id_type=MESH,
        )

    def start(self):
        for distance in sorted(range(1, self.parts), key=lambda k: -min(k, self.parts - k)):
            self.copy(distance).start()

    def arrive(self):
        for distance in range(1, self.parts):
            self.copy(distance).wait_recv()

    def drain(self):
        for distance in range(1, self.parts):
            self.copy(distance).wait_send()


def kernel(
    parts,
    field,
    stale_conv,
    stale_keys,
    stale_values,
    gain1,
    bias1,
    conv_weight,
    conv_bias,
    time_embed,
    gain2,
    bias2,
    w_query,
    w_keyvalue,
    w_out,
    to_group,
    from_group,
    same_group,
    out,
    wconv,
    wcat,
    wq,
    wkv,
    wo,
    act,
    kv_src,
    kv,
    stat_src,
    stat,
    st_src,
    st,
    nrm_src,
    nrm,
    hid_src,
    hid,
    load_sem,
    act_sem,
    kv_sem,
    x_send,
    x_recv,
):
    me = lax.axis_index("patch")
    rows, cols, channels = field.shape
    tokens = rows * cols
    share = channels // parts
    width = w_query.shape[1]
    positions = parts * tokens
    number = positions * (channels // GROUPS)

    loads = [
        pltpu.make_async_copy(source, target, load_sem.at[index])
        for index, (source, target) in enumerate(
            [(conv_weight, wconv), (w_query, wq), (w_keyvalue, wkv), (w_out, wo)]
        )
    ]
    for load in loads:
        load.start()

    barrier = pltpu.get_barrier_semaphore()
    for distance in range(1, parts):
        pl.semaphore_signal(
            barrier,
            inc=1,
            device_id={"patch": lax.rem(me + distance, parts)},
            device_id_type=MESH,
        )

    acts = [
        Gather(parts, me, act.at[i, me], act.at[i], *[act_sem.at[i, k] for k in range(4)])
        for i in range(STEPS + 1)
    ]
    kvs = [
        Gather(parts, me, source, kv.at[i], *[kv_sem.at[i, k] for k in range(4)])
        for i, source in enumerate([kv_src] + [kv.at[i, me] for i in range(STEPS - 1)])
    ]

    def exchange(kind, step, source, target, shared=False):
        return Exchange(
            parts, me, source, target, x_send.at[kind, step], x_recv.at[kind, step], shared
        )

    stats = [exchange(0, s, stat_src.at[s], stat.at[s], True) for s in range(STEPS)]
    states = [exchange(1, s, st_src.at[s], st.at[s]) for s in range(STEPS)]
    norms = [exchange(2, s, nrm_src.at[s], nrm.at[s]) for s in range(STEPS)]
    hiddens = [exchange(3, s, hid_src.at[s], hid.at[s]) for s in range(STEPS)]

    def block(values, index):
        return values[:, index * share : (index + 1) * share]

    def own_share(values):
        picked = jnp.zeros((values.shape[0], share), F32)
        for index in range(parts):
            picked = jnp.where(me == index, block(values, index), picked)
        return picked

    def send_stats(step, state):
        sums = exact_dot(moments(state), to_group[...])
        stat_src[step] = sums
        stat[step, me] = sums

    state = field[...].reshape(tokens, channels)
    send_stats(0, state)
    act[0, me] = stale_conv[...].reshape(tokens, channels)
    kv_src[...] = jnp.concatenate(
        [stale_keys[...].astype(F32), stale_values[...].astype(F32)], axis=1
    ).astype(BF16)

    pl.semaphore_wait(barrier, parts - 1)
    stats[0].start()
    acts[0].start()

    shifts = own_share(conv_bias[...] + time_embed[...])
    gain = own_share(gain2[...])
    bias = own_share(bias2[...])
    loads[0].wait()
    for tap in range(3):
        wcat[tap] = jnp.concatenate(
            [wconv[tap, k].astype(F32) for k in range(3)], axis=1
        ).astype(BF16)
    for load in loads[1:]:
        load.wait()

    column = lax.broadcasted_iota(jnp.int32, (positions, share), 0) % cols
    head_row = lax.broadcasted_iota(jnp.int32, (HEADS * tokens, width), 0) // tokens
    head_col = lax.broadcasted_iota(jnp.int32, (HEADS * tokens, width), 1) // HEAD_DIM
    on_head = head_row == head_col

    for step in range(STEPS):
        stats[step].arrive()
        average, scale = mean_and_scale(jnp.sum(stat[step], axis=0), number)
        spread = exact_dot(jnp.concatenate([average, scale], axis=0), from_group[...])
        centred = (state - spread[0:1]) * spread[1:2] * gain1[...] + bias1[...]
        act[step + 1, me] = (centred * jax.nn.sigmoid(centred)).astype(BF16)
        acts[step + 1].start()
        for index in range(parts):
            st_src[step, index] = block(state, index)
        st[step, me] = st_src[step, me]
        states[step].start()
        if step == 0:
            acts[0].forward()
            kvs[0].start()
        acts[step + 1].forward()
        if step == 0:
            acts[0].arrive()
        acts[step + 1].arrive()

        def piece(which, row):
            return act[which, row // rows, (row % rows) * cols : (row % rows + 1) * cols, :]

        whole = parts * rows
        nothing = jnp.zeros((cols, channels), BF16)
        conv = None
        for tap in range(3):
            pieces = []
            for row in range(whole):
                near = row + tap - 1
                if near < 0 or near >= whole:
                    pieces.append(nothing)
                else:
                    same = near // rows == row // rows
                    pieces.append(piece(step + 1 if same else step, near))
            term = jnp.dot(
                jnp.concatenate(pieces, axis=0), wcat[tap], preferred_element_type=F32
            )
            conv = term if conv is None else conv + term
        before = pltpu.roll(block(conv, 0), 1, 0)
        after = pltpu.roll(block(conv, 2), positions - 1, 0)
        conv = (
            block(conv, 1)
            + jnp.where(column == 0, 0.0, before)
            + jnp.where(column == cols - 1, 0.0, after)
        )
        states[step].arrive()
        hidden = st[step].reshape(positions, share) + (conv + shifts[step : step + 1])
        average, scale = mean_and_scale(exact_dot(moments(hidden), same_group[...]), number)
        normed = ((hidden - average) * scale * gain + bias).astype(BF16)
        nrm_src[step] = normed.reshape(parts, tokens, share)
        norms[step].start()
        hid_src[step] = hidden.reshape(parts, tokens, share)
        hiddens[step].start()
        nrm[step, me] = nrm_src[step, me]
        hid[step, me] = hid_src[step, me]
        if step == 0:
            kvs[0].forward()
        norms[step].arrive()
        mine = jnp.concatenate(
            [nrm[step, index].astype(F32) for index in range(parts)], axis=1
        ).astype(BF16)
        fresh = jnp.dot(mine, wkv[...], preferred_element_type=F32).astype(BF16)
        kv[step, me] = fresh
        if step + 1 < STEPS:
            kvs[step + 1].start()
        query = jnp.dot(mine, wq[...], preferred_element_type=F32).astype(BF16)
        query = jnp.concatenate([query] * HEADS, axis=0)
        query = jnp.where(on_head, query.astype(F32), 0.0).astype(BF16)
        if step > 0:
            kvs[step].forward()
        kvs[step].arrive()
        both = kv[step].reshape(positions, 2 * width)
        scores = lax.dot_general(
            query, both[:, :width], (((1,), (1,)), ((), ())), preferred_element_type=F32
        ) * HEAD_DIM ** (-0.5)
        expo = jnp.exp(scores - jnp.max(scores, axis=-1, keepdims=True))
        totals = jnp.sum(expo, axis=-1, keepdims=True)
        summed = jnp.dot(expo.astype(BF16), both, preferred_element_type=F32)[:, width:]
        summed = jnp.where(on_head, summed / totals, 0.0)
        attended = jnp.sum(summed.reshape(HEADS, tokens, width), axis=0).astype(BF16)
        mixed = jnp.dot(attended, wo[...], preferred_element_type=F32)
        hiddens[step].arrive()
        state = jnp.concatenate([hid[step, index] for index in range(parts)], axis=1) + mixed
        if step + 1 < STEPS:
            send_stats(step + 1, state)
            stats[step + 1].start()
        out[step] = state.reshape(rows, cols, channels)

    for started in acts + kvs + stats + states + norms + hiddens:
        started.drain()


def per_device(
    field,
    stale_conv_in,
    stale_keys,
    stale_values,
    norm1_gain,
    norm1_bias,
    conv_weight,
    conv_bias,
    time_embed,
    norm2_gain,
    norm2_bias,
    w_query,
    w_keyvalue,
    w_out,
):
    parts = lax.axis_size("patch")
    rows, cols, channels = field.shape
    tokens = rows * cols
    share = channels // parts
    width = w_query.shape[1]
    members = channels // GROUPS
    chips = parts // CORES
    group_of = np.arange(channels) // members
    to_group = (group_of[:, None] == np.arange(LANES)[None, :]).astype(np.float32)
    same_group = (group_of[:share, None] == group_of[None, :share]).astype(np.float32)
    vmem = pl.BlockSpec(memory_space=pltpu.VMEM)
    away = pl.BlockSpec(memory_space=pl.ANY)
    dma = pltpu.SemaphoreType.DMA
    return pl.pallas_call(
        functools.partial(kernel, parts),
        out_shape=jax.ShapeDtypeStruct((STEPS, rows, cols, channels), F32),
        in_specs=[vmem] * 6 + [away] + [vmem] * 4 + [away] * 3 + [vmem] * 3,
        out_specs=vmem,
        scratch_shapes=[
            pltpu.VMEM(conv_weight.shape, BF16),
            pltpu.VMEM((3, channels, 3 * share), BF16),
            pltpu.VMEM(w_query.shape, BF16),
            pltpu.VMEM(w_keyvalue.shape, BF16),
            pltpu.VMEM(w_out.shape, BF16),
            pltpu.VMEM((STEPS + 1, parts, tokens, channels), BF16),
            pltpu.VMEM((tokens, 2 * width), BF16),
            pltpu.VMEM((STEPS, parts, tokens, 2 * width), BF16),
            pltpu.VMEM((STEPS, 2, LANES), F32),
            pltpu.VMEM((STEPS, parts, 2, LANES), F32),
            pltpu.VMEM((STEPS, parts, tokens, share), F32),
            pltpu.VMEM((STEPS, parts, tokens, share), F32),
            pltpu.VMEM((STEPS, parts, tokens, share), BF16),
            pltpu.VMEM((STEPS, parts, tokens, share), BF16),
            pltpu.VMEM((STEPS, parts, tokens, share), F32),
            pltpu.VMEM((STEPS, parts, tokens, share), F32),
            dma((4,)),
            dma((STEPS + 1, 4, chips)),
            dma((STEPS, 4, chips)),
            dma((4, STEPS, parts)),
            dma((4, STEPS, parts)),
        ],
        compiler_params=pltpu.CompilerParams(
            collective_id=0, has_side_effects=True, vmem_limit_bytes=56 * 1024 * 1024
        ),
        cost_estimate=pl.CostEstimate(
            flops=2 * STEPS * parts * tokens * 9 * channels * share,
            bytes_accessed=2 * (9 * channels * share + 2 * channels * channels),
            transcendentals=0,
        ),
    )(
        field,
        stale_conv_in,
        stale_keys,
        stale_values,
        norm1_gain.reshape(1, -1),
        norm1_bias.reshape(1, -1),
        conv_weight,
        conv_bias.reshape(1, -1),
        time_embed,
        norm2_gain.reshape(1, -1),
        norm2_bias.reshape(1, -1),
        w_query,
        w_keyvalue,
        w_out,
        jnp.asarray(to_group, BF16),
        jnp.asarray(to_group.T, BF16),
        jnp.asarray(same_group, BF16),
    )


def solution(mesh):
    spread = ("req", "patch")
    return jax.shard_map(
        per_device,
        mesh=mesh,
        in_specs=(
            P(spread, None, None),
            P(spread, None, None),
            P(spread, None),
            P(spread, None),
            P(),
            P(),
            P(None, None, None, "patch"),
            P(),
            P("req", None),
            P(),
            P(),
            P(),
            P(),
            P(),
        ),
        out_specs=P(None, spread, None, None),
        check_vma=False,
    )
```

time: 195 us -> 60.8 us (0.31); the launches traced: 192 us -> 60.5 us
  blocking collectives: 163 us -> 0 us
  Pallas kernels: 0 us -> 48.8 us
  matrix products: 7.47 us -> 0 us
  starting transfers between devices: 6.88 us -> 0 us
  other arithmetic: 3.21 us -> 0 us
    all_gather x7 -> x0, blocking collectives: 108 us -> none  [the longest x2 33 us: per_device(): current_whole = lax.all_gather(activated, 'patch', axis=0, tiled=True)]
    psum x4 -> x0, blocking collectives: 54.9 us -> none  [group_norm(): lax.psum((jnp.sum(grouped, axis=(0, 2)), jnp.sum(grouped * grouped, axis=...]
    pallas_call x0 -> x1, Pallas kernels: none -> 48.8 us  [per_device(): pl.pallas_call(functools.partial(kernel, parts), out_shape=jax.ShapeDtype...]
    dot_general x28 -> x0, matrix products: 7.47 us -> none  [the longest x18 4.27 us: conv_rows(): jnp.dot(window, kernel[offset_row, offset_col], preferred_element_type=jn...]
    all_to_all x2 -> x0, starting transfers between devices: 6.88 us -> none  [per_device(): lax.all_to_all(partial_out, 'patch', split_axis=0, concat_axis=1, tiled=T...]
    reshape x4 -> x5, local copies, waits for them, and re-layouts: 0.4 us -> 6.43 us  [the longest x1 1.35 us: per_device(): norm1_gain.reshape(1, -1)]
    unnamed x26 -> x5, local copies, waits for them, and re-layouts: 0.95 us -> 5.21 us
    dynamic_update_slice x5 -> x0, local copies, waits for them, and re-layouts: 2.99 us -> none  [the longest x2 2.11 us: attend(): all_values = lax.dynamic_update_slice_in_dim(all_values, values, start, 0)]
  transfers between devices with their start and end apart: 2 -> 0, of which waited for: 0 -> 0; matrix products, arithmetic and copies ran while one was open for 1% -> 0% of each run, Pallas kernels for 0% -> 0%
where the time goes in v1:
time: 60.8 us; the launch traced here: 60.5 us
  Pallas kernels  48.8 us (80%)
  local copies, waits for them, and re-layouts  11.6 us (19%)
    pallas_call x1, Pallas kernels, per_device(): pl.pallas_call(functools.partial(kernel, parts), out_shape=jax.ShapeDtype...  48.8 us
    unnamed x5, local copies, waits for them, and re-layouts  5.21 us
    reshape x1, local copies, waits for them, and re-layouts, per_device(): norm1_gain.reshape(1, -1)  1.35 us
    reshape x1, local copies, waits for them, and re-layouts, per_device(): norm2_bias.reshape(1, -1)  1.28 us
    reshape x1, local copies, waits for them, and re-layouts, per_device(): norm1_bias.reshape(1, -1)  1.28 us
    reshape x1, local copies, waits for them, and re-layouts, per_device(): conv_bias.reshape(1, -1)  1.27 us
    reshape x1, local copies, waits for them, and re-layouts, per_device(): norm2_gain.reshape(1, -1)  1.26 us

profile of v1, /device:TPU:1, one launch (start us, length us, event | category | flops | bytes accessed | tf_op | source)
XLA Modules:
  0.0 60.5 jit_solution(10954765901974253079)
XLA Ops:
  0.0 0.0 copy-start
  0.0 1.3 %reshape.15.gain1 = f32[1,640]{1,0:T(1,128)} reshape(f32[640]{0:T(1024)} %param.21) | data formatting | bytes 5120 | tf_op jit(solution)/shard_map/reshape | solution.py:431
  1.4 1.3 %reshape.16.bias1 = f32[1,640]{1,0:T(1,128)} reshape(f32[640]{0:T(1024)} %param.22) | data formatting | bytes 5120 | tf_op jit(solution)/shard_map/reshape | solution.py:432
  2.6 1.3 %reshape.17.conv_bias = f32[1,640]{1,0:T(1,128)} reshape(f32[640]{0:T(1024)} %param.24) | data formatting | bytes 5120 | tf_op jit(solution)/shard_map/reshape | solution.py:434
  3.9 1.3 %reshape.18.gain2 = f32[1,640]{1,0:T(1,128)} reshape(f32[640]{0:T(1024)} %param.26) | data formatting | bytes 5120 | tf_op jit(solution)/shard_map/reshape | solution.py:436
  5.2 1.3 %reshape.19.bias2 = f32[1,640]{1,0:T(1,128)} reshape(f32[640]{0:T(1024)} %param.27) | data formatting | bytes 5120 | tf_op jit(solution)/shard_map/reshape | solution.py:437
  6.4 2.0 %copy.19.w_query = bf16[640,320]{1,0:T(8,128)(2,1)} copy(bf16[640,320]{0,1:T(8,128)(2,1)} %param.28) | data formatting | bytes 819200 | tf_op args[11]
  8.4 0.0 copy-done
  8.4 1.6 %copy.18.conv_weight = bf16[3,3,640,80]{3,2,1,0:T(8,128)(2,1)} copy(bf16[3,3,640,80]{2,3,1,0:T(8,128)(2,1)S(1)} %copy-done) | data formatting | bytes 1843200 | tf_op args[6]
  10.1 48.8 %shard_map.163 = f32[2,2,16,640]{3,2,1,0:T(8,128)} custom-call(f32[2,16,640]{2,1,0:T(8,128)} %field.1, bf16[2,16,640]{2,1,0:T(8,128)(2,1)} %stale_conv.1, bf16[32,320]{1,0:T(8,128)(2,1)} %stale_keys.1, bf16[32,320]{1,0:T(8,128)(2,1)} %stale_values.1, f32[1,640]{1,0:T(1,128)} %reshape.15.gain1, f32[1,640]{1,0:T(1,128)} %reshape.16.bias1, ...), custom_call_target="tpu_custom_call" | custom-call | flops 471859200 | bytes 2560000 | tf_op jit(solution)/shard_map/pallas_call | solution.py:390
  58.9 1.6 %copy.21 = f32[2,2,16,640]{3,2,1,0:T(8,128)} copy(f32[2,2,16,640]{3,2,1,0:T(8,128)} %shard_map.163) | data formatting | bytes 327680
Async XLA Ops:
  0.0 8.4 %copy-start = (bf16[3,3,640,80]{2,3,1,0:T(8,128)(2,1)S(1)}, bf16[3,3,640,80]{2,3,1,0:T(8,128)(2,1)}, u32[]{:S(2)}) copy-start(bf16[3,3,640,80]{2,3,1,0:T(8,128)(2,1)} %param.23) | copy-start | bytes 2764804

commit v2 on v1

--- a/solution.py
+++ b/solution.py
@@ -32,6 +32,12 @@
     rows = pair.shape[0]
     product = jnp.dot(split_rows(pair), zero_one, preferred_element_type=F32)
     return product[:rows] + product[rows : 2 * rows] + product[2 * rows :]
+
+
+def dot_transposed(left, right):
+    return lax.dot_general(
+        left, right, (((1,), (1,)), ((), ())), preferred_element_type=F32
+    )
 
 
 def moments(values):
@@ -159,7 +165,6 @@
     same_group,
     out,
     wconv,
-    wcat,
     wq,
     wkv,
     wo,
@@ -184,7 +189,7 @@
     rows, cols, channels = field.shape
     tokens = rows * cols
     share = channels // parts
-    width = w_query.shape[1]
+    width = w_query.shape[0]
     positions = parts * tokens
     number = positions * (channels // GROUPS)
 
@@ -250,14 +255,10 @@
     stats[0].start()
     acts[0].start()
 
-    shifts = own_share(conv_bias[...] + time_embed[...])
-    gain = own_share(gain2[...])
-    bias = own_share(bias2[...])
+    shifts = own_share(conv_bias[...][None, :] + time_embed[...])
+    gain = own_share(gain2[...][None, :])
+    bias = own_share(bias2[...][None, :])
     loads[0].wait()
-    for tap in range(3):
-        wcat[tap] = jnp.concatenate(
-            [wconv[tap, k].astype(F32) for k in range(3)], axis=1
-        ).astype(BF16)
     for load in loads[1:]:
         load.wait()
 
@@ -270,7 +271,7 @@
         stats[step].arrive()
         average, scale = mean_and_scale(jnp.sum(stat[step], axis=0), number)
         spread = exact_dot(jnp.concatenate([average, scale], axis=0), from_group[...])
-        centred = (state - spread[0:1]) * spread[1:2] * gain1[...] + bias1[...]
+        centred = (state - spread[0:1]) * spread[1:2] * gain1[...][None, :] + bias1[...][None, :]
         act[step + 1, me] = (centred * jax.nn.sigmoid(centred)).astype(BF16)
         acts[step + 1].start()
         for index in range(parts):
@@ -300,8 +301,8 @@
                 else:
                     same = near // rows == row // rows
                     pieces.append(piece(step + 1 if same else step, near))
-            term = jnp.dot(
-                jnp.concatenate(pieces, axis=0), wcat[tap], preferred_element_type=F32
+            term = dot_transposed(
+                jnp.concatenate(pieces, axis=0), wconv[tap].reshape(3 * share, channels)
             )
             conv = term if conv is None else conv + term
         before = pltpu.roll(block(conv, 0), 1, 0)
@@ -331,16 +332,14 @@
         kv[step, me] = fresh
         if step + 1 < STEPS:
             kvs[step + 1].start()
-        query = jnp.dot(mine, wq[...], preferred_element_type=F32).astype(BF16)
+        query = dot_transposed(mine, wq[...]).astype(BF16)
         query = jnp.concatenate([query] * HEADS, axis=0)
         query = jnp.where(on_head, query.astype(F32), 0.0).astype(BF16)
         if step > 0:
             kvs[step].forward()
         kvs[step].arrive()
         both = kv[step].reshape(positions, 2 * width)
-        scores = lax.dot_general(
-            query, both[:, :width], (((1,), (1,)), ((), ())), preferred_element_type=F32
-        ) * HEAD_DIM ** (-0.5)
+        scores = dot_transposed(query, both[:, :width]) * HEAD_DIM ** (-0.5)
         expo = jnp.exp(scores - jnp.max(scores, axis=-1, keepdims=True))
         totals = jnp.sum(expo, axis=-1, keepdims=True)
         summed = jnp.dot(expo.astype(BF16), both, preferred_element_type=F32)[:, width:]
@@ -393,9 +392,8 @@
         in_specs=[vmem] * 6 + [away] + [vmem] * 4 + [away] * 3 + [vmem] * 3,
         out_specs=vmem,
         scratch_shapes=[
-            pltpu.VMEM(conv_weight.shape, BF16),
-            pltpu.VMEM((3, channels, 3 * share), BF16),
-            pltpu.VMEM(w_query.shape, BF16),
+            pltpu.VMEM((3, 3, share, channels), BF16),
+            pltpu.VMEM((width, channels), BF16),
             pltpu.VMEM(w_keyvalue.shape, BF16),
             pltpu.VMEM(w_out.shape, BF16),
             pltpu.VMEM((STEPS + 1, parts, tokens, channels), BF16),
@@ -428,14 +426,14 @@
         stale_conv_in,
         stale_keys,
         stale_values,
-        norm1_gain.reshape(1, -1),
-        norm1_bias.reshape(1, -1),
-        conv_weight,
-        conv_bias.reshape(1, -1),
+        norm1_gain,
+        norm1_bias,
+        conv_weight.transpose(0, 1, 3, 2),
+        conv_bias,
         time_embed,
-        norm2_gain.reshape(1, -1),
-        norm2_bias.reshape(1, -1),
-        w_query,
+        norm2_gain,
+        norm2_bias,
+        w_query.T,
         w_keyvalue,
         w_out,
         jnp.asarray(to_group, BF16),

time: 60.8 us -> 50.7 us (0.83)
  local copies, waits for them, and re-layouts: 11.6 us -> 1.59 us
    reshape x5 -> x0, local copies, waits for them, and re-layouts: 6.43 us -> none  [the longest x1 1.35 us: per_device(): norm1_gain.reshape(1, -1)]
    unnamed x5 -> x1, local copies, waits for them, and re-layouts: 5.21 us -> 1.59 us
where the time goes in v2:
time: 50.7 us; the launch traced here: 50.6 us
  Pallas kernels  49 us (97%)
  local copies, waits for them, and re-layouts  1.59 us (3%)
    pallas_call x1, Pallas kernels, per_device(): pl.pallas_call(functools.partial(kernel, parts), out_shape=jax.ShapeDtype...  49 us
    unnamed x1, local copies, waits for them, and re-layouts  1.59 us

profile of v2, /device:TPU:1, one launch (start us, length us, event | category | flops | bytes accessed | tf_op | source)
XLA Modules:
  0.0 50.6 jit_solution(11139076912486405229)
XLA Ops:
  0.0 49.0 %shard_map.163 = f32[2,2,16,640]{3,2,1,0:T(8,128)} custom-call(f32[2,16,640]{2,1,0:T(8,128)} %field.1, bf16[2,16,640]{2,1,0:T(8,128)(2,1)} %stale_conv.1, bf16[32,320]{1,0:T(8,128)(2,1)} %stale_keys.1, bf16[32,320]{1,0:T(8,128)(2,1)} %stale_values.1, f32[640]{0:T(1024)} %gain1.1, f32[640]{0:T(1024)} %bias1.1, bf16[3,3,80,640]{3,2,1,0:T(8,128)(2,1)} %bitcast.2, ...), custom_call_target="tpu_custom_call" | custom-call | flops 471859200 | bytes 2560000 | tf_op jit(solution)/shard_map/pallas_call | solution.py:389
  49.0 1.6 %copy.19 = f32[2,2,16,640]{3,2,1,0:T(8,128)} copy(f32[2,2,16,640]{3,2,1,0:T(8,128)} %shard_map.163) | data formatting | bytes 327680

commit v3 on v2

--- a/solution.py
+++ b/solution.py
@@ -101,6 +101,18 @@
         for distance in range(1, self.chips):
             self.first(distance).wait_recv()
             self.second(distance).start()
+
+    def walk(self, use):
+        use(self.me)
+        self.first(0).wait_recv()
+        use(self.twin)
+        for distance in range(1, self.chips):
+            self.first(distance).wait_recv()
+            self.second(distance).start()
+            use(lax.rem(self.chip - distance + self.chips, self.chips) * CORES + self.core)
+        for distance in range(1, self.chips):
+            self.second(distance).wait_recv()
+            use(lax.rem(self.chip - distance + self.chips, self.chips) * CORES + 1 - self.core)
 
     def arrive(self):
         self.first(0).wait_recv()
@@ -171,16 +183,16 @@
     act,
     kv_src,
     kv,
-    stat_src,
     stat,
-    st_src,
-    st,
+    cen,
     nrm_src,
     nrm,
     hid_src,
     hid,
     load_sem,
     act_sem,
+    stat_sem,
+    cen_sem,
     kv_sem,
     x_send,
     x_recv,
@@ -211,10 +223,14 @@
             device_id_type=MESH,
         )
 
+    def gather(block_of, sems, i):
+        return Gather(parts, me, block_of.at[i, me], block_of.at[i], *[sems.at[i, k] for k in range(4)])
+
     acts = [
-        Gather(parts, me, act.at[i, me], act.at[i], *[act_sem.at[i, k] for k in range(4)])
-        for i in range(STEPS + 1)
+        Gather(parts, me, act.at[0, me], act.at[0], *[act_sem.at[k] for k in range(4)])
     ]
+    stats = [gather(stat, stat_sem, step) for step in range(STEPS)]
+    cens = [gather(cen, cen_sem, step) for step in range(STEPS)]
     kvs = [
         Gather(parts, me, source, kv.at[i], *[kv_sem.at[i, k] for k in range(4)])
         for i, source in enumerate([kv_src] + [kv.at[i, me] for i in range(STEPS - 1)])
@@ -225,10 +241,8 @@
             parts, me, source, target, x_send.at[kind, step], x_recv.at[kind, step], shared
         )
 
-    stats = [exchange(0, s, stat_src.at[s], stat.at[s], True) for s in range(STEPS)]
-    states = [exchange(1, s, st_src.at[s], st.at[s]) for s in range(STEPS)]
-    norms = [exchange(2, s, nrm_src.at[s], nrm.at[s]) for s in range(STEPS)]
-    hiddens = [exchange(3, s, hid_src.at[s], hid.at[s]) for s in range(STEPS)]
+    norms = [exchange(0, s, nrm_src.at[s], nrm.at[s]) for s in range(STEPS)]
+    hiddens = [exchange(1, s, hid_src.at[s], hid.at[s]) for s in range(STEPS)]
 
     def block(values, index):
         return values[:, index * share : (index + 1) * share]
@@ -239,52 +253,68 @@
             picked = jnp.where(me == index, block(values, index), picked)
         return picked
 
-    def send_stats(step, state):
-        sums = exact_dot(moments(state), to_group[...])
-        stat_src[step] = sums
+    def send_state(step, state):
+        sums = moments(state)
         stat[step, me] = sums
+        if step > 0:
+            stats[step].start()
+        cen[step, me] = (state - sums[0:1] * (1.0 / tokens)).astype(BF16)
+        if step > 0:
+            cens[step].start()
 
     state = field[...].reshape(tokens, channels)
-    send_stats(0, state)
+    send_state(0, state)
     act[0, me] = stale_conv[...].reshape(tokens, channels)
     kv_src[...] = jnp.concatenate(
         [stale_keys[...].astype(F32), stale_values[...].astype(F32)], axis=1
     ).astype(BF16)
 
     pl.semaphore_wait(barrier, parts - 1)
-    stats[0].start()
-    acts[0].start()
-
-    shifts = own_share(conv_bias[...][None, :] + time_embed[...])
+    for started in (stats[0], cens[0], acts[0], kvs[0]):
+        started.start()
+
+    row_shifts = conv_bias[...][None, :] + time_embed[...]
+    shifts = own_share(row_shifts)
     gain = own_share(gain2[...][None, :])
     bias = own_share(bias2[...][None, :])
     loads[0].wait()
     for load in loads[1:]:
         load.wait()
 
+    pick = jnp.where(
+        lax.broadcasted_iota(jnp.int32, (channels, share), 0) - me * share
+        == lax.broadcasted_iota(jnp.int32, (channels, share), 1),
+        1.0,
+        0.0,
+    ).astype(BF16)
     column = lax.broadcasted_iota(jnp.int32, (positions, share), 0) % cols
     head_row = lax.broadcasted_iota(jnp.int32, (HEADS * tokens, width), 0) // tokens
     head_col = lax.broadcasted_iota(jnp.int32, (HEADS * tokens, width), 1) // HEAD_DIM
     on_head = head_row == head_col
 
     for step in range(STEPS):
+        stats[step].forward()
         stats[step].arrive()
-        average, scale = mean_and_scale(jnp.sum(stat[step], axis=0), number)
+        sums = exact_dot(jnp.sum(stat[step], axis=0), to_group[...])
+        average, scale = mean_and_scale(sums, number)
         spread = exact_dot(jnp.concatenate([average, scale], axis=0), from_group[...])
-        centred = (state - spread[0:1]) * spread[1:2] * gain1[...][None, :] + bias1[...][None, :]
-        act[step + 1, me] = (centred * jax.nn.sigmoid(centred)).astype(BF16)
-        acts[step + 1].start()
-        for index in range(parts):
-            st_src[step, index] = block(state, index)
-        st[step, me] = st_src[step, me]
-        states[step].start()
+        slope = spread[1:2] * gain1[...][None, :]
+        average = spread[0:1]
+
+        def activate(which):
+            mean = stat[step, which][0:1] * (1.0 / tokens)
+            offset = (mean - average) * slope + bias1[...][None, :]
+            value = cen[step, which].astype(F32) * slope + offset
+            act[step + 1, which] = (value * jax.nn.sigmoid(value)).astype(BF16)
+
+        cens[step].walk(activate)
+        means = stat[step][:, 0, :] * (1.0 / tokens)
+        held = jnp.dot(
+            cen[step].reshape(positions, channels), pick, preferred_element_type=F32
+        ).reshape(parts, tokens, share) + exact_dot(means, pick)[:, None, :]
         if step == 0:
             acts[0].forward()
-            kvs[0].start()
-        acts[step + 1].forward()
-        if step == 0:
             acts[0].arrive()
-        acts[step + 1].arrive()
 
         def piece(which, row):
             return act[which, row // rows, (row % rows) * cols : (row % rows + 1) * cols, :]
@@ -312,13 +342,12 @@
             + jnp.where(column == 0, 0.0, before)
             + jnp.where(column == cols - 1, 0.0, after)
         )
-        states[step].arrive()
-        hidden = st[step].reshape(positions, share) + (conv + shifts[step : step + 1])
+        hidden = held.reshape(positions, share) + (conv + shifts[step : step + 1])
         average, scale = mean_and_scale(exact_dot(moments(hidden), same_group[...]), number)
         normed = ((hidden - average) * scale * gain + bias).astype(BF16)
         nrm_src[step] = normed.reshape(parts, tokens, share)
         norms[step].start()
-        hid_src[step] = hidden.reshape(parts, tokens, share)
+        hid_src[step] = conv.astype(BF16).reshape(parts, tokens, share)
         hiddens[step].start()
         nrm[step, me] = nrm_src[step, me]
         hid[step, me] = hid_src[step, me]
@@ -347,13 +376,15 @@
         attended = jnp.sum(summed.reshape(HEADS, tokens, width), axis=0).astype(BF16)
         mixed = jnp.dot(attended, wo[...], preferred_element_type=F32)
         hiddens[step].arrive()
-        state = jnp.concatenate([hid[step, index] for index in range(parts)], axis=1) + mixed
+        convolved = jnp.concatenate(
+            [hid[step, index].astype(F32) for index in range(parts)], axis=1
+        )
+        state = (state + (convolved + row_shifts[step : step + 1])) + mixed
         if step + 1 < STEPS:
-            send_stats(step + 1, state)
-            stats[step + 1].start()
+            send_state(step + 1, state)
         out[step] = state.reshape(rows, cols, channels)
 
-    for started in acts + kvs + stats + states + norms + hiddens:
+    for started in acts + kvs + stats + cens + norms + hiddens:
         started.drain()
 
 
@@ -399,19 +430,19 @@
             pltpu.VMEM((STEPS + 1, parts, tokens, channels), BF16),
             pltpu.VMEM((tokens, 2 * width), BF16),
             pltpu.VMEM((STEPS, parts, tokens, 2 * width), BF16),
-            pltpu.VMEM((STEPS, 2, LANES), F32),
-            pltpu.VMEM((STEPS, parts, 2, LANES), F32),
-            pltpu.VMEM((STEPS, parts, tokens, share), F32),
-            pltpu.VMEM((STEPS, parts, tokens, share), F32),
+            pltpu.VMEM((STEPS, parts, 2, channels), F32),
+            pltpu.VMEM((STEPS, parts, tokens, channels), BF16),
             pltpu.VMEM((STEPS, parts, tokens, share), BF16),
             pltpu.VMEM((STEPS, parts, tokens, share), BF16),
-            pltpu.VMEM((STEPS, parts, tokens, share), F32),
-            pltpu.VMEM((STEPS, parts, tokens, share), F32),
+            pltpu.VMEM((STEPS, parts, tokens, share), BF16),
+            pltpu.VMEM((STEPS, parts, tokens, share), BF16),
             dma((4,)),
-            dma((STEPS + 1, 4, chips)),
+            dma((4, chips)),
             dma((STEPS, 4, chips)),
-            dma((4, STEPS, parts)),
-            dma((4, STEPS, parts)),
+            dma((STEPS, 4, chips)),
+            dma((STEPS, 4, chips)),
+            dma((2, STEPS, parts)),
+            dma((2, STEPS, parts)),
         ],
         compiler_params=pltpu.CompilerParams(
             collective_id=0, has_side_effects=True, vmem_limit_bytes=56 * 1024 * 1024

time: 50.7 us -> 45.9 us (0.905)
  Pallas kernels: 49 us -> 44.1 us
    pallas_call x1, Pallas kernels: 49 us -> 44.1 us  [per_device(): pl.pallas_call(functools.partial(kernel, parts), out_shape=jax.ShapeDtype...]
where the time goes in v3:
time: 45.9 us; the launch traced here: 45.7 us
  Pallas kernels  44.1 us (96%)
  local copies, waits for them, and re-layouts  1.59 us (3%)
    pallas_call x1, Pallas kernels, per_device(): pl.pallas_call(functools.partial(kernel, parts), out_shape=jax.ShapeDtype...  44.1 us
    unnamed x1, local copies, waits for them, and re-layouts  1.59 us

profile of v3, /device:TPU:1, one launch (start us, length us, event | category | flops | bytes accessed | tf_op | source)
XLA Modules:
  0.0 45.7 jit_solution(8499383368872550162)
XLA Ops:
  0.0 44.1 %shard_map.163 = f32[2,2,16,640]{3,2,1,0:T(8,128)} custom-call(f32[2,16,640]{2,1,0:T(8,128)} %field.1, bf16[2,16,640]{2,1,0:T(8,128)(2,1)} %stale_conv.1, bf16[32,320]{1,0:T(8,128)(2,1)} %stale_keys.1, bf16[32,320]{1,0:T(8,128)(2,1)} %stale_values.1, f32[640]{0:T(1024)} %gain1.1, f32[640]{0:T(1024)} %bias1.1, bf16[3,3,80,640]{3,2,1,0:T(8,128)(2,1)} %bitcast.2, ...), custom_call_target="tpu_custom_call" | custom-call | flops 471859200 | bytes 2560000 | tf_op jit(solution)/shard_map/pallas_call | solution.py:420
  44.1 1.6 %copy.19 = f32[2,2,16,640]{3,2,1,0:T(8,128)} copy(f32[2,2,16,640]{3,2,1,0:T(8,128)} %shard_map.163) | data formatting | bytes 327680

commit v4 on v3

--- a/solution.py
+++ b/solution.py
@@ -270,7 +270,7 @@
     ).astype(BF16)
 
     pl.semaphore_wait(barrier, parts - 1)
-    for started in (stats[0], cens[0], acts[0], kvs[0]):
+    for started in (stats[0], cens[0], acts[0]):
         started.start()
 
     row_shifts = conv_bias[...][None, :] + time_embed[...]
@@ -313,6 +313,7 @@
             cen[step].reshape(positions, channels), pick, preferred_element_type=F32
         ).reshape(parts, tokens, share) + exact_dot(means, pick)[:, None, :]
         if step == 0:
+            kvs[0].start()
             acts[0].forward()
             acts[0].arrive()
 

time: 45.9 us -> 43.7 us (0.952)
  Pallas kernels: 44.1 us -> 41.9 us
    pallas_call x1, Pallas kernels: 44.1 us -> 41.9 us  [per_device(): pl.pallas_call(functools.partial(kernel, parts), out_shape=jax.ShapeDtype...]
where the time goes in v4:
time: 43.7 us; the launch traced here: 43.5 us
  Pallas kernels  41.9 us (96%)
  local copies, waits for them, and re-layouts  1.59 us (4%)
    pallas_call x1, Pallas kernels, per_device(): pl.pallas_call(functools.partial(kernel, parts), out_shape=jax.ShapeDtype...  41.9 us
    unnamed x1, local copies, waits for them, and re-layouts  1.59 us

profile of v4, /device:TPU:1, one launch (start us, length us, event | category | flops | bytes accessed | tf_op | source)
XLA Modules:
  0.0 43.5 jit_solution(5316874619753650339)
XLA Ops:
  0.0 41.9 %shard_map.163 = f32[2,2,16,640]{3,2,1,0:T(8,128)} custom-call(f32[2,16,640]{2,1,0:T(8,128)} %field.1, bf16[2,16,640]{2,1,0:T(8,128)(2,1)} %stale_conv.1, bf16[32,320]{1,0:T(8,128)(2,1)} %stale_keys.1, bf16[32,320]{1,0:T(8,128)(2,1)} %stale_values.1, f32[640]{0:T(1024)} %gain1.1, f32[640]{0:T(1024)} %bias1.1, bf16[3,3,80,640]{3,2,1,0:T(8,128)(2,1)} %bitcast.2, ...), custom_call_target="tpu_custom_call" | custom-call | flops 471859200 | bytes 2560000 | tf_op jit(solution)/shard_map/pallas_call | solution.py:421
  41.9 1.6 %copy.19 = f32[2,2,16,640]{3,2,1,0:T(8,128)} copy(f32[2,2,16,640]{3,2,1,0:T(8,128)} %shard_map.163) | data formatting | bytes 327680
